TPU v7x, 32 devices: a whole 2x2x4 slice. The times are simulated.
32 devices in a mesh: fsdp: 8 (over y, x, core), rep: 4 (over z).
Axes of the slice: x: 2, y: 2, z: 4, core: 2. Of those that a mesh axis runs over, the one named last changes fastest.
Arguments:
- tokens: bfloat16 [16384, 1024], P(('fsdp', 'rep')), may hold values from -6 to 6
- seq_lengths: int32 [32, 4], P(('fsdp', 'rep')), may hold values from 1 to 320, 512 in all within a row
- attn_norm: bfloat16 [1024], P(('fsdp', 'rep')), may hold values from 0.25 to 1.75
- q_weight: bfloat16 [1024, 2048], P(('fsdp', 'rep')), may hold values from -0.1875 to 0.1875
- k_weight: bfloat16 [1024, 1024], P(('fsdp', 'rep')), may hold values from -0.1875 to 0.1875
- v_weight: bfloat16 [1024, 1024], P(('fsdp', 'rep')), may hold values from -0.1875 to 0.1875
- o_weight: bfloat16 [2048, 1024], P(('fsdp', 'rep')), may hold values from -1 to 1
- head_gains: bfloat16 [2, 128], replicated, may hold values from 0.25 to 1.75
- mlp_norm: bfloat16 [1024], P(('fsdp', 'rep')), may hold values from 0.25 to 1.75
- gate_weight: bfloat16 [1024, 3072], P(('fsdp', 'rep')), may hold values from -0.1875 to 0.1875
- up_weight: bfloat16 [1024, 3072], P(('fsdp', 'rep')), may hold values from -0.1875 to 0.1875
- down_weight: bfloat16 [3072, 1024], P(('fsdp', 'rep')), may hold values from -0.109375 to 0.109375
- cotangent: bfloat16 [16384, 1024], P(('fsdp', 'rep')), may hold values from -6 to 6
Outputs:
- layer_out: bfloat16 [16384, 1024], P(('fsdp', 'rep'))
- input_grad: float32 [16384, 1024], P(('fsdp', 'rep'))
- attn_norm_grad: float32 [1024], P(('fsdp', 'rep'))
- q_grad: float32 [1024, 2048], P(('fsdp', 'rep'))
- k_grad: float32 [1024, 1024], P(('fsdp', 'rep'))
- v_grad: float32 [1024, 1024], P(('fsdp', 'rep'))
- o_grad: float32 [2048, 1024], P(('fsdp', 'rep'))
- head_gains_grad: float32 [2, 128], replicated
- mlp_norm_grad: float32 [1024], P(('fsdp', 'rep'))
- gate_grad: float32 [1024, 3072], P(('fsdp', 'rep'))
- up_grad: float32 [1024, 3072], P(('fsdp', 'rep'))
- down_grad: float32 [3072, 1024], P(('fsdp', 'rep'))
Inputs may be any that keep to these rules, and one draw needn't show every extreme that they name: `seq_lengths`: each row holds the lengths of the 4 sequences packed in order on one device; a row sums to 512, and its longest is exactly 320.
All inputs are finite; a program needn't handle non-finite values.
Results may differ from a plain program's by a relative error of at most 0.014.
Values may be sent and summed in bfloat16 or wider, within the bound.
A program may use at most 256 MiB of HBM per device.

v0:
```python
import jax
import jax.numpy as jnp
from jax import lax
from jax.sharding import PartitionSpec as P

EPSILON = 1e-06
ROPE_BASE = 1000000.0


def halve(values):
    return values.astype(jnp.bfloat16)


def round_trip(values):
    return lax.optimization_barrier(values.astype(jnp.bfloat16)).astype(jnp.float32)


def same_value(values):
    return values


def narrow_pass(kept, grad):
    return (grad,)


def grad_keep(values):
    return (values, None)


def dot_forward(left, right):
    return jnp.dot(halve(left), halve(right), preferred_element_type=jnp.float32)


def dot_keep(left, right):
    return (dot_forward(left, right), (halve(left), halve(right)))


def dot_back(kept, grad):
    left_low, right_low = kept
    grad_low = halve(grad)
    left_grad = jnp.dot(grad_low, right_low.T, preferred_element_type=jnp.float32)
    right_grad = jnp.dot(left_low.T, grad_low, preferred_element_type=jnp.float32)
    return (left_grad, right_grad)


def score_forward(query_block, key_block):
    return jnp.einsum(
        "tgd,sd->gts", halve(query_block), halve(key_block), preferred_element_type=jnp.float32
    )


def score_keep(query_block, key_block):
    return (score_forward(query_block, key_block), (halve(query_block), halve(key_block)))


def score_back(kept, grad):
    query_low, key_low = kept
    grad_low = halve(grad)
    query_grad = jnp.einsum("gts,sd->tgd", grad_low, key_low, preferred_element_type=jnp.float32)
    key_grad = jnp.einsum("gts,tgd->sd", grad_low, query_low, preferred_element_type=jnp.float32)
    return (query_grad, key_grad)


def value_forward(prob_block, value_block):
    return jnp.einsum(
        "gts,sd->tgd", halve(prob_block), halve(value_block), preferred_element_type=jnp.float32
    )


def value_keep(prob_block, value_block):
    return (value_forward(prob_block, value_block), (halve(prob_block), halve(value_block)))


def value_back(kept, grad):
    prob_low, value_low = kept
    grad_low = halve(grad)
    prob_grad = jnp.einsum("tgd,sd->gts", grad_low, value_low, preferred_element_type=jnp.float32)
    value_grad = jnp.einsum("gts,tgd->sd", prob_low, grad_low, preferred_element_type=jnp.float32)
    return (prob_grad, value_grad)


def build_helpers():
    narrow = jax.custom_vjp(round_trip)

    def narrow_keep(values):
        return (narrow(values), None)

    narrow.defvjp(narrow_keep, narrow_pass)
    narrow_back = jax.custom_vjp(same_value)

    def grad_narrow(kept, grad):
        return (narrow(grad),)

    narrow_back.defvjp(grad_keep, grad_narrow)
    plain_dot = jax.custom_vjp(dot_forward)
    plain_dot.defvjp(dot_keep, dot_back)
    score_product = jax.custom_vjp(score_forward)
    score_product.defvjp(score_keep, score_back)
    value_product = jax.custom_vjp(value_forward)
    value_product.defvjp(value_keep, value_back)
    return (narrow, narrow_back, plain_dot, score_product, value_product)


def normalize(values, gain_row):
    return (
        values * lax.rsqrt(jnp.mean(values * values, axis=-1, keepdims=True) + EPSILON) * gain_row
    )


def rotary(values, cosine_table, sine_table):
    half_width = values.shape[-1] // 2
    first_half = values[..., :half_width]
    second_half = values[..., half_width:]
    return jnp.concatenate(
        [
            first_half * cosine_table - second_half * sine_table,
            second_half * cosine_table + first_half * sine_table,
        ],
        axis=-1,
    )


def layout(lengths_row, row_count):
    seq_ends = jnp.cumsum(lengths_row)
    seq_starts = seq_ends - lengths_row
    places = jnp.arange(row_count, dtype=jnp.int32)
    segment = jnp.sum((places[:, None] >= seq_ends[None, :]).astype(jnp.int32), axis=1)
    owned_by = segment[:, None] == jnp.arange(lengths_row.shape[0], dtype=jnp.int32)[None, :]
    position = places - jnp.sum(jnp.where(owned_by, seq_starts[None, :], 0), axis=1)
    allowed = (segment[:, None] == segment[None, :]) & (places[None, :] <= places[:, None])
    return (position, allowed)


def layer(tokens, weights, lengths_row, helpers):
    narrow, narrow_back, plain_dot, score_product, value_product = helpers
    (
        attn_norm,
        q_weight,
        k_weight,
        v_weight,
        o_weight,
        head_gains,
        mlp_norm,
        gate_weight,
        up_weight,
        down_weight,
    ) = weights
    row_count = tokens.shape[0]
    head_size = head_gains.shape[1]
    kv_heads = k_weight.shape[1] // head_size
    q_heads = q_weight.shape[1] // head_size
    group_size = q_heads // kv_heads
    position, allowed = layout(lengths_row, row_count)
    frequency = ROPE_BASE ** (-(jnp.arange(head_size // 2, dtype=jnp.float32) * 2.0 / head_size))
    angles = position.astype(jnp.float32)[:, None] * frequency[None, :]
    cosine_table = jnp.cos(angles)[:, None, :]
    sine_table = jnp.sin(angles)[:, None, :]
    normed = narrow(normalize(tokens, attn_norm))
    queries = narrow_back(plain_dot(normed, q_weight)).reshape(row_count, q_heads, head_size)
    keys_raw = narrow_back(plain_dot(normed, k_weight)).reshape(row_count, kv_heads, head_size)
    values_in = narrow(narrow_back(plain_dot(normed, v_weight))).reshape(
        row_count, kv_heads, head_size
    )
    queries = narrow(rotary(normalize(queries, head_gains[0]), cosine_table, sine_table))
    keys = narrow(rotary(normalize(keys_raw, head_gains[1]), cosine_table, sine_table))
    query_groups = queries.reshape(row_count, kv_heads, group_size, head_size).transpose(1, 0, 2, 3)
    key_groups = keys.transpose(1, 0, 2)
    value_groups = values_in.transpose(1, 0, 2)

    def attend(operands):
        query_block, key_block, value_block = operands
        scores = score_product(query_block, key_block) * head_size ** (-0.5)
        scores = narrow_back(scores)
        scores = jnp.where(allowed[None], scores, -1e30)
        weights_soft = jnp.exp(scores - jnp.max(scores, axis=-1, keepdims=True))
        probabilities = narrow(weights_soft / jnp.sum(weights_soft, axis=-1, keepdims=True))
        return value_product(probabilities, value_block)

    attended = lax.map(jax.checkpoint(attend), (query_groups, key_groups, value_groups))
    attended = attended.transpose(1, 0, 2, 3).reshape(row_count, q_heads * head_size)
    attended = narrow(narrow_back(attended))
    branch = narrow_back(plain_dot(attended, o_weight))
    middle = tokens + branch
    normed_two = narrow(normalize(middle, mlp_norm))
    gate_value = narrow_back(plain_dot(normed_two, gate_weight))
    up_value = narrow_back(plain_dot(normed_two, up_weight))
    hidden = narrow(jax.nn.silu(gate_value) * up_value)
    return middle + narrow_back(plain_dot(hidden, down_weight))


def assemble(attention_set, head_gains, mlp_set):
    return tuple(
        (
            item.astype(jnp.float32)
            for item in (
                attention_set[0],
                attention_set[1],
                attention_set[2],
                attention_set[3],
                attention_set[4],
                head_gains,
                mlp_set[0],
                mlp_set[1],
                mlp_set[2],
                mlp_set[3],
            )
        )
    )


def local(
    tokens,
    seq_lengths,
    attn_norm,
    q_weight,
    k_weight,
    v_weight,
    o_weight,
    head_gains,
    mlp_norm,
    gate_weight,
    up_weight,
    down_weight,
    cotangent,
):
    helpers = build_helpers()
    lengths_row = seq_lengths[0]
    inputs = tokens.astype(jnp.float32)
    attention_set = (
        lax.all_gather(attn_norm, ("fsdp", "rep"), axis=0, tiled=True),
        lax.all_gather(q_weight, ("fsdp", "rep"), axis=0, tiled=True),
        lax.all_gather(k_weight, ("fsdp", "rep"), axis=0, tiled=True),
        lax.all_gather(v_weight, ("fsdp", "rep"), axis=0, tiled=True),
        lax.all_gather(o_weight, ("fsdp", "rep"), axis=0, tiled=True),
    )
    mlp_set = (
        lax.all_gather(mlp_norm, ("fsdp", "rep"), axis=0, tiled=True),
        lax.all_gather(gate_weight, ("fsdp", "rep"), axis=0, tiled=True),
        lax.all_gather(up_weight, ("fsdp", "rep"), axis=0, tiled=True),
        lax.all_gather(down_weight, ("fsdp", "rep"), axis=0, tiled=True),
    )
    weights = assemble(attention_set, head_gains, mlp_set)

    def local_layer(layer_inputs, layer_weights):
        return layer(layer_inputs, layer_weights, lengths_row, helpers)

    outputs = local_layer(inputs, weights)
    attention_again = (
        lax.all_gather(attn_norm, ("fsdp", "rep"), axis=0, tiled=True),
        lax.all_gather(q_weight, ("fsdp", "rep"), axis=0, tiled=True),
        lax.all_gather(k_weight, ("fsdp", "rep"), axis=0, tiled=True),
        lax.all_gather(v_weight, ("fsdp", "rep"), axis=0, tiled=True),
        lax.all_gather(o_weight, ("fsdp", "rep"), axis=0, tiled=True),
    )
    mlp_again = (
        lax.all_gather(mlp_norm, ("fsdp", "rep"), axis=0, tiled=True),
        lax.all_gather(gate_weight, ("fsdp", "rep"), axis=0, tiled=True),
        lax.all_gather(up_weight, ("fsdp", "rep"), axis=0, tiled=True),
        lax.all_gather(down_weight, ("fsdp", "rep"), axis=0, tiled=True),
    )
    weights_again = assemble(attention_again, head_gains, mlp_again)
    unused_out, pullback = jax.vjp(local_layer, inputs, weights_again)
    input_grad, weight_grads = pullback(cotangent.astype(jnp.float32))
    attention_terms = (
        weight_grads[0],
        weight_grads[1],
        weight_grads[2],
        weight_grads[3],
        weight_grads[4],
    )
    mlp_terms = (weight_grads[6], weight_grads[7], weight_grads[8], weight_grads[9])
    attention_sums = (
        lax.psum_scatter(attention_terms[0], ("fsdp", "rep"), scatter_dimension=0, tiled=True),
        lax.psum_scatter(attention_terms[1], ("fsdp", "rep"), scatter_dimension=0, tiled=True),
        lax.psum_scatter(attention_terms[2], ("fsdp", "rep"), scatter_dimension=0, tiled=True),
        lax.psum_scatter(attention_terms[3], ("fsdp", "rep"), scatter_dimension=0, tiled=True),
        lax.psum_scatter(attention_terms[4], ("fsdp", "rep"), scatter_dimension=0, tiled=True),
    )
    mlp_sums = (
        lax.psum_scatter(mlp_terms[0], ("fsdp", "rep"), scatter_dimension=0, tiled=True),
        lax.psum_scatter(mlp_terms[1], ("fsdp", "rep"), scatter_dimension=0, tiled=True),
        lax.psum_scatter(mlp_terms[2], ("fsdp", "rep"), scatter_dimension=0, tiled=True),
        lax.psum_scatter(mlp_terms[3], ("fsdp", "rep"), scatter_dimension=0, tiled=True),
    )
    head_sums = lax.psum(weight_grads[5], ("fsdp", "rep"))
    return (
        outputs.astype(jnp.bfloat16),
        input_grad,
        attention_sums[0],
        attention_sums[1],
        attention_sums[2],
        attention_sums[3],
        attention_sums[4],
        head_sums,
        mlp_sums[0],
        mlp_sums[1],
        mlp_sums[2],
        mlp_sums[3],
    )


def solution(mesh):
    placed = (
        P(("fsdp", "rep"), None),
        P(("fsdp", "rep"), None),
        P(("fsdp", "rep")),
        P(("fsdp", "rep"), None),
        P(("fsdp", "rep"), None),
        P(("fsdp", "rep"), None),
        P(("fsdp", "rep"), None),
        P(),
        P(("fsdp", "rep")),
        P(("fsdp", "rep"), None),
        P(("fsdp", "rep"), None),
        P(("fsdp", "rep"), None),
        P(("fsdp", "rep"), None),
    )
    return jax.shard_map(
        local,
        mesh=mesh,
        in_specs=placed,
        out_specs=(
            P(("fsdp", "rep"), None),
            P(("fsdp", "rep"), None),
            P(("fsdp", "rep")),
            P(("fsdp", "rep"), None),
            P(("fsdp", "rep"), None),
            P(("fsdp", "rep"), None),
            P(("fsdp", "rep"), None),
            P(),
            P(("fsdp", "rep")),
            P(("fsdp", "rep"), None),
            P(("fsdp", "rep"), None),
            P(("fsdp", "rep"), None),
        ),
        check_vma=False,
    )
```

profile of v0, /device:TPU:0, one launch (start us, length us, event | category | flops | bytes accessed | tf_op | source)
XLA Modules:
  0.0 1758.0 jit_solution(14241361948181263405)
XLA Ops:
  18.3 42.1 %all-reduce.11 = (bf16[1024]{0:T(1024)(128)(2,1)S(1)}, bf16[1024]{0:T(1024)(128)(2,1)S(1)}) all-reduce(bf16[1024]{0:T(1024)(128)(2,1)S(1)} %dynamic-update-slice, bf16[1024]{0:T(1024)(128)(2,1)S(1)} %dynamic-update-slice.1), channel_id=1, replica_groups=mesh['fsdp'=8,'rep'=4] {'fsdp','rep'}, use_global_device_ids=true, to_apply=%add.6 | all-reduce | flops 2048 | bytes 8192
  84.4 44.4 %all-gather.8.cloned.1.call-done = bf16[1024,1024]{1,0:T(8,128)(2,1)} async-done(((bf16[32,1024]{1,0:T(8,128)(2,1)}), bf16[1024,1024]{1,0:T(8,128)(2,1)}) %all-gather.8.cloned.1.call-update) | async-done | bytes 2097168 | tf_op jit(solution)/shard_map/all_gather | solution.py:233
  135.0 57.8 %all-gather.12.cloned.1.call-done = bf16[1024,2048]{1,0:T(8,128)(2,1)} async-done(((bf16[32,2048]{1,0:T(8,128)(2,1)}), bf16[1024,2048]{1,0:T(8,128)(2,1)}) %all-gather.12.cloned.1.call-update) | async-done | bytes 4194320 | tf_op jit(solution)/shard_map/all_gather | solution.py:231
  211.4 34.1 %while.43 = (s32[]{:T(128)}, bf16[8,512,2,128]{1,3,2,0:T(8,128)(2,1)}, bf16[8,512,128]{1,2,0:T(8,128)(2,1)}, bf16[8,512,128]{2,1,0:T(8,128)(2,1)}, bf16[8,512,2,...) while((s32[]{:T(128)}, bf16[8,512,2,128]{1,3,2,0:T(8,128)(2,1)}, ...), condition=%wide.region_14.15_spmd.clone, body=%wide.region_11.14_spmd.clone.sunk | while | flops 271581696 | bytes 7612493 | solution.py:179
  245.5 35.6 %while.42 = (s32[]{:T(128)}, bf16[8,512,2,128]{1,3,2,0:T(8,128)(2,1)}, bf16[8,512,128]{1,2,0:T(8,128)(2,1)}, bf16[8,512,128]{2,1,0:T(8,128)(2,1)}, bf16[8,512,2,...) while((s32[]{:T(128)}, bf16[8,512,2,128]{1,3,2,0:T(8,128)(2,1)}, ...), condition=%wide.region_9.10_spmd.clone, body=%wide.region_6.9_spmd.clone.sunk | while | flops 272368128 | bytes 7876685 | solution.py:179
  293.8 33.3 %all-gather.16.cloned.1.call-done = bf16[1024,3072]{1,0:T(8,128)(2,1)} async-done(((bf16[32,3072]{1,0:T(8,128)(2,1)}), bf16[1024,3072]{1,0:T(8,128)(2,1)}) %all-gather.16.cloned.1.call-update) | async-done | bytes 6291472 | tf_op jit(solution)/shard_map/all_gather | solution.py:238
  327.1 9.2 fusion.121
  336.2 61.7 %all-gather.20.cloned.1.call-done = bf16[3072,1024]{1,0:T(8,128)(2,1)} async-done(((bf16[96,1024]{1,0:T(8,128)(2,1)}), bf16[3072,1024]{1,0:T(8,128)(2,1)}) %all-gather.20.cloned.1.call-update) | async-done | bytes 6291472 | tf_op jit(solution)/shard_map/all_gather | solution.py:240
  397.9 8.3 fusion.122
  406.2 62.7 %all-gather.18.cloned.1.call-done = bf16[1024,3072]{1,0:T(8,128)(2,1)} async-done(((bf16[32,3072]{1,0:T(8,128)(2,1)}), bf16[1024,3072]{1,0:T(8,128)(2,1)}) %all-gather.18.cloned.1.call-update) | async-done | bytes 6291472 | tf_op jit(solution)/shard_map/all_gather | solution.py:239
  468.9 11.8 multiply_convert_fusion.3
  510.3 80.2 %while.44 = (s32[]{:T(128)}, f32[8,512,2,128]{1,3,2,0:T(8,128)}, f32[8,512,128]{1,2,0:T(8,128)}, bf16[8,512,128]{1,2,0:T(8,128)(2,1)}, bf16[8,512,2,128]{3,1,2,0...) while((s32[]{:T(128)}, f32[8,512,2,128]{1,3,2,0:T(8,128)}, ...), condition=%wide.region_23.24_spmd.clone, body=%wide.region_17.23_spmd.clone.sunk | while | flops 689176576 | bytes 28010640 | solution.py:179
  604.1 10.2 fusion.130
  614.4 10.2 fusion.131
  652.0 12.5 multiply_reduce_fusion
  666.4 7.7 fusion.92
  682.0 8.4 fusion.132
  702.4 40.0 %all-reduce.10 = (f32[1024]{0:T(1024)S(1)}, f32[2,128]{1,0:T(2,128)}, f32[1024]{0:T(1024)S(1)}) all-reduce(f32[1024]{0:T(1024)S(1)} %get-tuple-element.445, f32[2,128]{1,0:T(2,128)S(1)} %pad_add_fusion.2, f32[1024]{0:T(1024)S(1)} %copy-done.48), channel_id=2, replica_groups=mesh['fsdp'=8,'rep'=4] {'fsdp','rep'}, use_global_device_ids=true, to_apply=%region_28.29.clone | all-reduce | flops 2304 | bytes 18432
  762.8 131.9 %reduce-scatter.12.cloned.1.call-done = f32[32,1024]{1,0:T(8,128)} async-done(((f32[1024,1024]{1,0:T(8,128)}), f32[32,1024]{1,0:T(8,128)}) %reduce-scatter.12.cloned.1.call-update) | async-done | bytes 131088 | tf_op jit(solution)/shard_map/reduce_scatter | solution.py:276
  894.7 160.3 %reduce-scatter.16.cloned.1.call-done = f32[32,3072]{1,0:T(8,128)} async-done(((f32[1024,3072]{1,0:T(8,128)}), f32[32,3072]{1,0:T(8,128)}) %reduce-scatter.16.cloned.1.call-update) | async-done | bytes 393232 | tf_op jit(solution)/shard_map/reduce_scatter | solution.py:281
  1054.9 162.4 %reduce-scatter.18.cloned.1.call-done = f32[32,3072]{1,0:T(8,128)} async-done(((f32[1024,3072]{1,0:T(8,128)}), f32[32,3072]{1,0:T(8,128)}) %reduce-scatter.18.cloned.1.call-update) | async-done | bytes 393232 | tf_op jit(solution)/shard_map/reduce_scatter | solution.py:282
  1217.4 187.7 %reduce-scatter.14.cloned.1.call-done = f32[64,1024]{1,0:T(8,128)} async-done(((f32[2048,1024]{1,0:T(8,128)}), f32[64,1024]{1,0:T(8,128)}) %reduce-scatter.14.cloned.1.call-update) | async-done | bytes 262160 | tf_op jit(solution)/shard_map/reduce_scatter | solution.py:277
  1405.1 186.4 %reduce-scatter.8.cloned.1.call-done = f32[32,2048]{1,0:T(8,128)} async-done(((f32[1024,2048]{1,0:T(8,128)}), f32[32,2048]{1,0:T(8,128)}) %reduce-scatter.8.cloned.1.call-update) | async-done | bytes 262160 | tf_op jit(solution)/shard_map/reduce_scatter | solution.py:274
  1591.4 159.5 %reduce-scatter.20.cloned.1.call-done = f32[96,1024]{1,0:T(8,128)} async-done(((f32[3072,1024]{1,0:T(8,128)}), f32[96,1024]{1,0:T(8,128)}) %reduce-scatter.20.cloned.1.call-update) | async-done | bytes 393232 | tf_op jit(solution)/shard_map/reduce_scatter | solution.py:283
  (425 shorter events, 333.6 us)
Async XLA Ops:
  7.2 63.3 %all-gather.10.cloned.1.call-start = ((), (), s32[]{:S(2)}) async-start(), calls=%async_computation.8 | async-start | bytes 2162688 | tf_op jit(solution)/shard_map/all_gather | solution.py:232
  7.9 120.9 %all-gather.8.cloned.1.call-start = ((), (), s32[]{:S(2)}) async-start(), calls=%async_computation.7 | async-start | bytes 2162688 | tf_op jit(solution)/shard_map/all_gather | solution.py:233
  8.7 184.2 %all-gather.12.cloned.1.call-start = ((), (), s32[]{:S(2)}) async-start(), calls=%async_computation.9 | async-start | bytes 4325376 | tf_op jit(solution)/shard_map/all_gather | solution.py:231
  9.4 271.7 %all-gather.14.cloned.1.call-start = ((), (), s32[]{:S(2)}) async-start(), calls=%async_computation.10 | async-start | bytes 4325376 | tf_op jit(solution)/shard_map/all_gather | solution.py:234
  10.0 317.1 %all-gather.16.cloned.1.call-start = ((), (), s32[]{:S(2)}) async-start(), calls=%async_computation.11 | async-start | bytes 6488064 | tf_op jit(solution)/shard_map/all_gather | solution.py:238
  10.6 387.3 %all-gather.20.cloned.1.call-start = ((), (), s32[]{:S(2)}) async-start(), calls=%async_computation.13 | async-start | bytes 6488064 | tf_op jit(solution)/shard_map/all_gather | solution.py:240
  11.1 457.7 %all-gather.18.cloned.1.call-start = ((), (), s32[]{:S(2)}) async-start(), calls=%async_computation.12 | async-start | bytes 6488064 | tf_op jit(solution)/shard_map/all_gather | solution.py:239
  11.9 750.9 %reduce-scatter.10.cloned.1.call-start = ((), (), s32[]{:S(2)}) async-start(), calls=%async_computation.15 | async-start | bytes 4325376 | tf_op jit(solution)/shard_map/reduce_scatter | solution.py:275
  13.5 47.0 %copy-start.7 = (bf16[512,1024]{1,0:T(8,128)(2,1)S(1)}, bf16[512,1024]{1,0:T(8,128)(2,1)}, u32[]{:S(2)}) copy-start(bf16[512,1024]{1,0:T(8,128)(2,1)} %param.19) | copy-start | bytes 3145732
  16.7 44.4 %copy-start.57 = (s32[1,4]{1,0:T(1,128)S(1)}, s32[1,4]{1,0:T(1,128)}, u32[]{:S(2)}) copy-start(s32[1,4]{1,0:T(1,128)} %param.20) | copy-start | bytes 52
  61.1 141.0 %copy-start.41 = (f32[128]{0:T(128)}, f32[128]{0:T(128)S(1)}, u32[]{:S(2)}) copy-start(f32[128]{0:T(128)S(1)} %get-tuple-element.528) | copy-start | bytes 1540
  63.1 143.2 %copy-start.14 = (f32[512,64]{1,0:T(8,128)}, f32[512,64]{1,0:T(8,128)S(1)}, u32[]{:S(2)}) copy-start(f32[512,64]{1,0:T(8,128)S(1)} %copy.162) | copy-start | bytes 393220
  83.1 49.0 %copy-start.10 = (bf16[512,8,128]{0,2,1:T(8,128)(2,1)}, bf16[512,8,128]{0,2,1:T(8,128)(2,1)S(1)}, u32[]{:S(2)}) copy-start(bf16[512,8,128]{0,2,1:T(8,128)(2,1)S(1)} %pad_maximum_fusion.1) | copy-start | bytes 3145732
  133.5 59.4 %copy-start.23 = (bf16[512,1024]{1,0:T(8,128)(2,1)S(1)}, bf16[512,1024]{1,0:T(8,128)(2,1)}, u32[]{:S(2)}) copy-start(bf16[512,1024]{1,0:T(8,128)(2,1)} %copy-done.22) | copy-start | bytes 3145732
  293.8 104.1 %copy-start.13 = (bf16[512,1024]{1,0:T(8,128)(2,1)S(1)}, bf16[512,1024]{1,0:T(8,128)(2,1)}, u32[]{:S(2)}) copy-start(bf16[512,1024]{1,0:T(8,128)(2,1)} %param.31) | copy-start | bytes 3145732
  510.3 80.2 %copy-start.21 = (f32[512,64]{0,1:T(8,128)S(1)}, f32[512,64]{0,1:T(8,128)}, u32[]{:S(2)}) copy-start(f32[512,64]{0,1:T(8,128)} %copy-done.19) | copy-start | bytes 393220
  598.7 295.9 %reduce-scatter.12.cloned.1.call-start = ((), (), s32[]{:S(2)}) async-start(), calls=%async_computation.16 | async-start | bytes 4325376 | tf_op jit(solution)/shard_map/reduce_scatter | solution.py:276
  603.7 451.3 %reduce-scatter.16.cloned.1.call-start = ((), (), s32[]{:S(2)}) async-start(), calls=%async_computation.18 | async-start | bytes 12976128 | tf_op jit(solution)/shard_map/reduce_scatter | solution.py:281
  614.4 603.0 %reduce-scatter.18.cloned.1.call-start = ((), (), s32[]{:S(2)}) async-start(), calls=%async_computation.19 | async-start | bytes 12976128 | tf_op jit(solution)/shard_map/reduce_scatter | solution.py:282
  624.7 780.4 %reduce-scatter.14.cloned.1.call-start = ((), (), s32[]{:S(2)}) async-start(), calls=%async_computation.17 | async-start | bytes 8650752 | tf_op jit(solution)/shard_map/reduce_scatter | solution.py:277
  632.1 959.3 %reduce-scatter.8.cloned.1.call-start = ((), (), s32[]{:S(2)}) async-start(), calls=%async_computation.14 | async-start | bytes 8650752 | tf_op jit(solution)/shard_map/reduce_scatter | solution.py:274
  681.7 1069.3 %reduce-scatter.20.cloned.1.call-start = ((), (), s32[]{:S(2)}) async-start(), calls=%async_computation.20 | async-start | bytes 12976128 | tf_op jit(solution)/shard_map/reduce_scatter | solution.py:283
  698.2 45.3 %copy-start.40 = (f32[512]{0:T(512)S(1)}, f32[512]{0:T(512)}, u32[]{:S(2)}) copy-start(f32[512]{0:T(512)} %copy-done.39) | copy-start | bytes 6148
  698.2 45.3 %copy-start.43 = (f32[512]{0:T(512)S(1)}, f32[512]{0:T(512)}, u32[]{:S(2)}) copy-start(f32[512]{0:T(512)} %get-tuple-element.536) | copy-start | bytes 6148
  (54 other events, 310.8 us)
Sparse Core Ops, SparseCore 0:
  10.9 59.5 all-gather.9
  73.4 55.3 all-gather.7
  131.8 60.9 all-gather.11
  195.7 60.6 all-gather.13
  259.1 67.9 all-gather.15
  329.8 68.0 all-gather.19
  400.8 68.0 all-gather.17
  598.9 146.8 reduce-scatter.9
  748.6 146.0 reduce-scatter.11
  901.1 153.7 reduce-scatter.15
  1062.6 154.7 reduce-scatter.17
  1220.1 184.9 reduce-scatter.13
  1407.9 183.4 reduce-scatter.7
  1597.9 153.0 reduce-scatter.19
where the time goes:
time: 1770 us; the launch traced here: 1760 us
  waiting for transfers between devices  1260 us (71%)
  matrix products  239 us (14%)
  local copies, waits for them, and re-layouts  82.5 us (5%)
  blocking collectives  82.1 us (5%)
  other arithmetic  77.8 us (4%)
    reduce_scatter x1, waiting for transfers between devices, local(): lax.psum_scatter(attention_terms[4], ('fsdp', 'rep'), scatter_dimension=0...  188 us
    reduce_scatter x1, waiting for transfers between devices, local(): lax.psum_scatter(attention_terms[1], ('fsdp', 'rep'), scatter_dimension=0...  186 us
    reduce_scatter x1, waiting for transfers between devices, local(): lax.psum_scatter(mlp_terms[2], ('fsdp', 'rep'), scatter_dimension=0, tile...  162 us
    reduce_scatter x1, waiting for transfers between devices, local(): lax.psum_scatter(mlp_terms[1], ('fsdp', 'rep'), scatter_dimension=0, tile...  160 us
    reduce_scatter x1, waiting for transfers between devices, local(): lax.psum_scatter(mlp_terms[3], ('fsdp', 'rep'), scatter_dimension=0, tile...  160 us
    reduce_scatter x1, waiting for transfers between devices, local(): lax.psum_scatter(attention_terms[3], ('fsdp', 'rep'), scatter_dimension=0...  132 us
    unnamed x2, blocking collectives  82.1 us
    all_gather x1, waiting for transfers between devices, local(): lax.all_gather(up_weight, ('fsdp', 'rep'), axis=0, tiled=True)  62.7 us
  transfers between devices with their start and end apart: 14, of which 12 were waited for; matrix products, arithmetic and copies ran while one was open for 15% of the time, Pallas kernels for 0%

commit v1 on v0

v1 whole, which is shorter than its diff:
```python
import functools

import jax
import jax.numpy as jnp
from jax import lax
from jax.experimental import pallas as pl
from jax.experimental.pallas import tpu as pltpu
from jax.sharding import PartitionSpec as P

EPSILON = 1e-06
ROPE_BASE = 1000000.0
AXES = ("fsdp", "rep")
ROWS = 256


def low(values):
    return values.astype(jnp.bfloat16)


def high(values):
    return values.astype(jnp.float32)


def dot(left, right, dims):
    return lax.dot_general(left, right, (dims, ((), ())), preferred_element_type=jnp.float32)


NN = ((1,), (0,))
NT = ((1,), (1,))
TN = ((0,), (0,))


def gather(block):
    return lax.all_gather(block, AXES, axis=0, tiled=True)


def scatter_sum(values):
    return lax.psum_scatter(values, AXES, scatter_dimension=0, tiled=True)


def head_norm_rope(raw, gain, cosine, sine):
    rate = lax.rsqrt(jnp.mean(raw * raw, axis=-1, keepdims=True) + EPSILON)
    unit = raw * rate
    normed = unit * gain
    return unit, rate, low(normed * cosine + pltpu.roll(normed, raw.shape[1] // 2, 1) * sine)


def head_norm_rope_back(grad, unit, rate, gain, cosine, sine):
    grad = grad * cosine - pltpu.roll(grad, grad.shape[1] // 2, 1) * sine
    gain_grad = jnp.sum(grad * unit, axis=0, keepdims=True)
    scaled = grad * gain
    return rate * (scaled - unit * jnp.mean(unit * scaled, axis=-1, keepdims=True)), gain_grad


def probabilities(query, key, start, first, scale):
    scores = dot(query, key, NT) * scale
    row = lax.broadcasted_iota(jnp.int32, scores.shape, 0) + first
    column = lax.broadcasted_iota(jnp.int32, scores.shape, 1)
    scores = jnp.where((column <= row) & (column >= start), scores, -1e30)
    soft = jnp.exp(scores - jnp.max(scores, axis=-1, keepdims=True))
    return soft * (1.0 / jnp.sum(soft, axis=-1, keepdims=True))


def attention_kernel(group, qkv_ref, cosine_ref, sine_ref, gains_ref, start_ref, out_ref):
    size = gains_ref.shape[1]
    count = qkv_ref.shape[0]
    scale = size**-0.5
    cosine, sine = cosine_ref[...], sine_ref[...]
    key_at, value_at = group * size, (group + 1) * size
    key = head_norm_rope(qkv_ref[:, key_at:value_at], gains_ref[1:2], cosine, sine)[2]
    value = low(qkv_ref[:, value_at:])
    for head in range(group):
        span = slice(head * size, (head + 1) * size)
        query = head_norm_rope(qkv_ref[:, span], gains_ref[0:1], cosine, sine)[2]
        for first in range(0, count, ROWS):
            last = first + ROWS
            prob = probabilities(
                query[first:last], key[:last], start_ref[first:last], first, scale
            )
            out_ref[first:last, span] = low(dot(low(prob), value[:last], NN))


def attention_back_kernel(
    group,
    qkv_ref,
    cosine_ref,
    sine_ref,
    gains_ref,
    start_ref,
    out_ref,
    dout_ref,
    grad_ref,
    gain_grad_ref,
    dkey_ref,
    dvalue_ref,
    dquery_ref,
):
    size = gains_ref.shape[1]
    count = qkv_ref.shape[0]
    scale = size**-0.5
    cosine, sine = cosine_ref[...], sine_ref[...]
    key_at, value_at = group * size, (group + 1) * size

    @pl.when(pl.program_id(0) == 0)
    def _():
        gain_grad_ref[...] = jnp.zeros_like(gain_grad_ref)

    key_unit, key_rate, key = head_norm_rope(
        qkv_ref[:, key_at:value_at], gains_ref[1:2], cosine, sine
    )
    value = low(qkv_ref[:, value_at:])
    dkey_ref[...] = jnp.zeros_like(dkey_ref)
    dvalue_ref[...] = jnp.zeros_like(dvalue_ref)
    for head in range(group):
        span = slice(head * size, (head + 1) * size)
        query_unit, query_rate, query = head_norm_rope(
            qkv_ref[:, span], gains_ref[0:1], cosine, sine
        )
        dout = dout_ref[:, span]
        delta = jnp.sum(high(dout) * high(out_ref[:, span]), axis=-1, keepdims=True)
        for first in range(0, count, ROWS):
            last = first + ROWS
            prob = probabilities(
                query[first:last], key[:last], start_ref[first:last], first, scale
            )
            prob = low(prob)
            dprob = dot(dout[first:last], value[:last], NT)
            dscore = low(high(prob) * (dprob - delta[first:last]) * scale)
            dquery_ref[first:last] = dot(dscore, key[:last], NN)
            dkey_ref[:last] += dot(dscore, query[first:last], TN)
            dvalue_ref[:last] += dot(prob, dout[first:last], TN)
        dquery, gain_grad = head_norm_rope_back(
            dquery_ref[...], query_unit, query_rate, gains_ref[0:1], cosine, sine
        )
        grad_ref[:, span] = low(dquery)
        gain_grad_ref[0:1] += gain_grad
    dkey, gain_grad = head_norm_rope_back(
        dkey_ref[...], key_unit, key_rate, gains_ref[1:2], cosine, sine
    )
    grad_ref[:, key_at:value_at] = low(dkey)
    grad_ref[:, value_at:] = low(dvalue_ref[...])
    gain_grad_ref[1:2] += gain_grad


def attention_specs(count, size, width, wide):
    whole = lambda shape: pl.BlockSpec(shape, lambda step: (0, 0))
    return [
        pl.BlockSpec((count, wide), lambda step: (0, step)),
        whole((count, size)),
        whole((count, size)),
        whole((2, size)),
        whole((count, 1)),
    ]


def attention(qkv, cosine, sine, gains, start, group):
    count, size = cosine.shape
    wide = (group + 2) * size
    heads = qkv.shape[1] // wide
    return pl.pallas_call(
        functools.partial(attention_kernel, group),
        grid=(heads,),
        out_shape=jax.ShapeDtypeStruct((count, heads * group * size), jnp.bfloat16),
        in_specs=attention_specs(count, size, group, wide),
        out_specs=pl.BlockSpec((count, group * size), lambda step: (0, step)),
        compiler_params=pltpu.CompilerParams(vmem_limit_bytes=32 * 2**20),
        cost_estimate=pl.CostEstimate(
            flops=3 * heads * group * count * count * size,
            bytes_accessed=qkv.size * 4 + count * heads * group * size * 2,
            transcendentals=heads * group * count * count,
        ),
        name="attention",
    )(qkv, cosine, sine, gains, start)


def attention_back(qkv, cosine, sine, gains, start, out, dout, group):
    count, size = cosine.shape
    wide = (group + 2) * size
    heads = qkv.shape[1] // wide
    side = pl.BlockSpec((count, group * size), lambda step: (0, step))
    return pl.pallas_call(
        functools.partial(attention_back_kernel, group),
        grid=(heads,),
        out_shape=[
            jax.ShapeDtypeStruct(qkv.shape, jnp.bfloat16),
            jax.ShapeDtypeStruct((8, size), jnp.float32),
        ],
        in_specs=attention_specs(count, size, group, wide) + [side, side],
        out_specs=[
            pl.BlockSpec((count, wide), lambda step: (0, step)),
            pl.BlockSpec((8, size), lambda step: (0, 0)),
        ],
        scratch_shapes=[pltpu.VMEM((count, size), jnp.float32)] * 3,
        compiler_params=pltpu.CompilerParams(vmem_limit_bytes=32 * 2**20),
        cost_estimate=pl.CostEstimate(
            flops=8 * heads * group * count * count * size,
            bytes_accessed=qkv.size * 6 + count * heads * group * size * 4,
            transcendentals=heads * group * count * count,
        ),
        name="attention_back",
    )(qkv, cosine, sine, gains, start, out, dout)


def layout(lengths_row, row_count):
    ends = jnp.cumsum(lengths_row)
    places = jnp.arange(row_count, dtype=jnp.int32)
    passed = places[:, None] >= ends[None, :]
    return jnp.max(jnp.where(passed, ends[None, :], 0), axis=1)


def rates(values):
    return lax.rsqrt(jnp.mean(values * values, axis=-1, keepdims=True) + EPSILON)


def norm_back(values, rate, gain, grad):
    scaled = grad * gain
    mean = jnp.mean(values * scaled, axis=-1, keepdims=True)
    gain_grad = jnp.sum(grad * values * rate, axis=0)
    return rate * scaled - values * (rate * rate * rate) * mean, gain_grad


def grouped(q_part, k_part, v_part, kv_heads):
    rows = q_part.shape[0]
    parts = [item.reshape(rows, kv_heads, -1) for item in (q_part, k_part, v_part)]
    return jnp.concatenate(parts, axis=2).reshape(rows, -1)


def local(
    tokens,
    seq_lengths,
    attn_norm,
    q_weight,
    k_weight,
    v_weight,
    o_weight,
    head_gains,
    mlp_norm,
    gate_weight,
    up_weight,
    down_weight,
    cotangent,
):
    count = tokens.shape[0]
    size = head_gains.shape[1]
    kv_heads = k_weight.shape[1] // size
    group = q_weight.shape[1] // k_weight.shape[1]
    hidden = gate_weight.shape[1]
    own = attn_norm.shape[0]

    norms = gather(jnp.stack([attn_norm, mlp_norm], axis=1))
    gain_one, gain_two = high(norms[:, 0]), high(norms[:, 1])
    qkv_weight = gather(grouped(q_weight, k_weight, v_weight, kv_heads))
    out_weight = gather(o_weight)
    pair_weight = gather(jnp.concatenate([gate_weight, up_weight], axis=1))
    back_weight = gather(down_weight)

    start = layout(seq_lengths[0], count)
    position = jnp.arange(count, dtype=jnp.int32) - start
    frequency = ROPE_BASE ** (-(jnp.arange(size // 2, dtype=jnp.float32) * 2.0 / size))
    angles = position.astype(jnp.float32)[:, None] * frequency[None, :]
    cosine, sine = jnp.cos(angles), jnp.sin(angles)
    cosine = jnp.concatenate([cosine, cosine], axis=1)
    sine = jnp.concatenate([-sine, sine], axis=1)
    gains = high(head_gains)
    tables = (cosine, sine, gains, start[:, None])

    inputs = high(tokens)
    rate_one = rates(inputs)
    normed_one = low(inputs * rate_one * gain_one)
    qkv = dot(normed_one, qkv_weight, NN)
    attended = attention(qkv, *tables, group)
    middle = inputs + dot(attended, out_weight, NN)
    rate_two = rates(middle)
    normed_two = low(middle * rate_two * gain_two)
    pair = dot(normed_two, pair_weight, NN)
    gate, up = pair[:, :hidden], pair[:, hidden:]
    gate_sigmoid = jax.nn.sigmoid(gate)
    gate_silu = gate * gate_sigmoid
    mixed = low(gate_silu * up)
    layer_out = low(middle + dot(mixed, back_weight, NN))

    down_sum = scatter_sum(low(dot(mixed, cotangent, TN)))
    dmixed = dot(cotangent, back_weight, NT)
    dgate = low(dmixed * up * (gate_sigmoid + gate_silu * (1.0 - gate_sigmoid)))
    dup = low(dmixed * gate_silu)
    dpair = jnp.concatenate([dgate, dup], axis=1)
    pair_sum = scatter_sum(low(dot(normed_two, dpair, TN)))
    dnormed_two = dot(dpair, pair_weight, NT)
    dmiddle, mlp_norm_grad = norm_back(middle, rate_two, gain_two, dnormed_two)
    dmiddle = high(cotangent) + dmiddle
    dbranch = low(dmiddle)
    out_sum = scatter_sum(low(dot(attended, dbranch, TN)))
    dattended = low(dot(dbranch, out_weight, NT))
    dqkv, gains_grad = attention_back(qkv, *tables, attended, dattended, group)
    qkv_sum = scatter_sum(low(dot(normed_one, dqkv, TN)))
    dnormed_one = dot(dqkv, qkv_weight, NT)
    dinputs, attn_norm_grad = norm_back(inputs, rate_one, gain_one, dnormed_one)
    input_grad = dmiddle + dinputs

    small = lax.psum(
        jnp.concatenate([attn_norm_grad, mlp_norm_grad, gains_grad[:2].reshape(-1)]), AXES
    )
    width = attn_norm_grad.shape[0]
    place = (lax.axis_index("fsdp") * lax.axis_size("rep") + lax.axis_index("rep")) * own
    attn_norm_sum = lax.dynamic_slice(small, (place,), (own,))
    mlp_norm_sum = lax.dynamic_slice(small, (width + place,), (own,))
    gains_sum = small[2 * width :].reshape(2, size)

    qkv_sum = high(qkv_sum).reshape(own, kv_heads, -1)
    q_sum = qkv_sum[:, :, : group * size].reshape(own, -1)
    k_sum = qkv_sum[:, :, group * size : (group + 1) * size].reshape(own, -1)
    v_sum = qkv_sum[:, :, (group + 1) * size :].reshape(own, -1)
    pair_sum = high(pair_sum)
    return (
        layer_out,
        input_grad,
        attn_norm_sum,
        q_sum,
        k_sum,
        v_sum,
        high(out_sum),
        gains_sum,
        mlp_norm_sum,
        pair_sum[:, :hidden],
        pair_sum[:, hidden:],
        high(down_sum),
    )


def solution(mesh):
    split, line = P(AXES, None), P(AXES)
    return jax.shard_map(
        local,
        mesh=mesh,
        in_specs=(
            split, split, line, split, split, split, split, P(), line, split, split, split, split
        ),
        out_specs=(
            split, split, line, split, split, split, split, P(), line, split, split, split
        ),
        check_vma=False,
    )
```

time: 1770 us -> 991 us (0.56)
  waiting for transfers between devices: 1260 us -> 653 us
  matrix products: 239 us -> 111 us
  other arithmetic: 77.8 us -> 13.7 us
  local copies, waits for them, and re-layouts: 82.5 us -> 21.6 us
  Pallas kernels: 0 us -> 57.3 us
  blocking collectives: 82.1 us -> 110 us
    reduce_scatter x7 -> x4, waiting for transfers between devices: 988 us -> 471 us  [scatter_sum(): return lax.psum_scatter(values, AXES, scatter_dimension=0, tiled=True)]
    dot_general x80 -> x12, matrix products: 207 us -> 111 us  [dot(): lax.dot_general(left, right, (dims, ((), ())), preferred_element_type=jnp...]
    all_gather x7 -> x4, waiting for transfers between devices: 266 us -> 181 us  [gather(): return lax.all_gather(block, AXES, axis=0, tiled=True)]
    unnamed x2 -> x0, blocking collectives: 82.1 us -> none
    all_gather x0 -> x1, blocking collectives: none -> 69.8 us  [gather(): return lax.all_gather(block, AXES, axis=0, tiled=True)]
    pallas_call x0 -> x2, Pallas kernels: none -> 57.3 us  [the longest x1 31.3 us: attention_back(): pl.pallas_call(functools.partial(attention_back_kernel, group), grid=(hea...]
    psum x0 -> x1, blocking collectives: none -> 40 us  [local(): lax.psum(jnp.concatenate([attn_norm_grad, mlp_norm_grad, gains_grad[:2].r...]
    sub x16 -> x0, matrix products: 32.5 us -> none  [attend(): weights_soft = jnp.exp(scores - jnp.max(scores, axis=-1, keepdims=True))]
  transfers between devices with their start and end apart: 14 -> 8, of which waited for: 12 -> 8; matrix products, arithmetic and copies ran while one was open for 15% -> 10% of each run, Pallas kernels for 0% -> 6%
where the time goes in v1:
time: 991 us; the launch traced here: 982 us
  waiting for transfers between devices  653 us (66%)
  matrix products  111 us (11%)
  blocking collectives  110 us (11%)
  Pallas kernels  57.3 us (6%)
  local copies, waits for them, and re-layouts  21.6 us (2%)
  between operations  14.6 us (1%)
  other arithmetic  13.7 us (1%)
    reduce_scatter x4, waiting for transfers between devices, scatter_sum(): return lax.psum_scatter(values, AXES, scatter_dimension=0, tiled=True)  471 us
    all_gather x4, waiting for transfers between devices, gather(): return lax.all_gather(block, AXES, axis=0, tiled=True)  181 us
    dot_general x12, matrix products, dot(): lax.dot_general(left, right, (dims, ((), ())), preferred_element_type=jnp...  111 us
    all_gather x1, blocking collectives, gather(): return lax.all_gather(block, AXES, axis=0, tiled=True)  69.8 us
    psum x1, blocking collectives, local(): lax.psum(jnp.concatenate([attn_norm_grad, mlp_norm_grad, gains_grad[:2].r...  40 us
    pallas_call x1, Pallas kernels, attention_back(): pl.pallas_call(functools.partial(attention_back_kernel, group), grid=(hea...  31.3 us
    pallas_call x1, Pallas kernels, attention(): pl.pallas_call(functools.partial(attention_kernel, group), grid=(heads,),...  26 us
  transfers between devices with their start and end apart: 8, of which 8 were waited for; matrix products, arithmetic and copies ran while one was open for 10% of the time, Pallas kernels for 6%

profile of v1, /device:TPU:0, one launch (start us, length us, event | category | flops | bytes accessed | tf_op | source)
XLA Modules:
  0.0 981.6 jit_solution(946111026624963576)
XLA Ops:
  14.1 69.8 %all-gather = bf16[32,32,2]{1,2,0:T(2,128)(2,1)S(1)} all-gather(bf16[1,32,2]{1,2,0:T(2,128)(2,1)S(1)} %maximum_bitcast_fusion), channel_id=1, replica_groups=mesh['fsdp'=8,'rep'=4] {'fsdp','rep'}, dimensions={0}, use_global_device_ids=true | all-gather | bytes 4224 | tf_op jit(solution)/shard_map/all_gather | solution.py:34
  86.1 5.8 all-gather.6.cloned.1.call-done
  91.9 7.2 fusion.13.qkv_ref
  99.1 26.0 %attention.1.out_ref = bf16[512,2048]{1,0:T(8,128)(2,1)S(1)} custom-call(f32[512,4096]{1,0:T(8,128)S(1)} %fusion.13.qkv_ref, f32[512,128]{1,0:T(8,128)S(1)} %get-tuple-element.42.cosine_ref, f32[512,128]{1,0:T(8,128)S(1)} %get-tuple-element.43.sine_ref, f32[2,128]{1,0:T(2,128)S(1)} %convert_element_type.87.gains_ref, s32[512,1]{1,0:T(8,128)S(1)} %copy.32.start_ref), custom_call_target="tpu_custom_call" | custom-call | flops 1610612736 | bytes 10485760 | tf_op jit(solution)/shard_map/attention/pallas_call | solution.py:160
  128.3 27.3 %all-gather.8.cloned.1.call-done = bf16[2048,1024]{1,0:T(8,128)(2,1)} async-done(((bf16[64,1024]{1,0:T(8,128)(2,1)}), bf16[2048,1024]{1,0:T(8,128)(2,1)}) %all-gather.8.cloned.1.call-update) | async-done | bytes 4194320 | tf_op jit(solution)/shard_map/all_gather | solution.py:34
  155.7 6.2 multiply_reduce_fusion.2
  161.9 91.8 %all-gather.10.cloned.1.call-done = bf16[1024,6144]{1,0:T(8,128)(2,1)} async-done(((bf16[32,6144]{1,0:T(8,128)(2,1)}), bf16[1024,6144]{1,0:T(8,128)(2,1)}) %all-gather.10.cloned.1.call-update) | async-done | bytes 12582928 | tf_op jit(solution)/shard_map/all_gather | solution.py:34
  253.7 14.5 %fusion.18 = f32[512,6144]{1,0:T(8,128)} fusion(bf16[1024,6144]{1,0:T(8,128)(2,1)} %all-gather.10.cloned.1.call-done, f32[512,1024]{1,0:T(8,128)} %get-tuple-element.39, f32[1024]{0:T(1024)S(1)} %bitcast.74, f32[512]{0:T(512)S(1)} %get-tuple-element.37), kind=kOutput, calls=%fused_computation.63 | convolution fusion | flops 6444023808 | bytes 27269120 | tf_op jit(solution)/shard_map/dot_general | solution.py:25
  268.3 56.0 %all-gather.12.cloned.1.call-done = bf16[3072,1024]{1,0:T(8,128)(2,1)} async-done(((bf16[96,1024]{1,0:T(8,128)(2,1)}), bf16[3072,1024]{1,0:T(8,128)(2,1)}) %all-gather.12.cloned.1.call-update) | async-done | bytes 6291472 | tf_op jit(solution)/shard_map/all_gather | solution.py:34
  324.3 12.6 %multiply_convert_fusion.1 = (bf16[512,3072]{1,0:T(8,128)(2,1)}, bf16[512,3072]{1,0:T(8,128)(2,1)}, bf16[512,3072]{1,0:T(8,128)(2,1)}) fusion(f32[512,6144]{1,0:T(8,128)} %fusion.18, bf16[512,1024]{1,0:T(8,128)(2,1)} %param.25, bf16[3072,1024]{1,0:T(8,128)(2,1)} %all-gather.12.cloned.1.call-done), kind=kOutput, calls=%fused_computation.4 | convolution fusion | flops 3243245568 | bytes 29360128 | tf_op jit(solution)/shard_map/dot_general | solution.py:25
  337.0 14.5 %multiply_reduce_fusion = (f32[1024]{0:T(1024)S(1)}, f32[512]{0:T(512)S(1)}, f32[512,1024]{1,0:T(8,128)}) fusion(f32[512,1024]{1,0:T(8,128)} %get-tuple-element.39, f32[512]{0:T(512)S(1)} %get-tuple-element.37, f32[1024]{0:T(1024)S(1)} %bitcast.75, bf16[1024,6144]{1,0:T(8,128)(2,1)} %all-gather.10.cloned.1.call-done, ...), kind=kOutput, calls=%fused_computation.27 | convolution fusion | flops 6458178048 | bytes 23080960 | tf_op jit(solution)/shard_map/dot_general | solution.py:25
  355.9 4.4 convolution_convert_fusion.3
  360.3 8.3 convolution_convert_fusion.2
  368.7 5.2 convolution_convert_fusion.4.dout_ref
  377.4 31.3 %attention_back.1 = (bf16[512,4096]{1,0:T(8,128)(2,1)S(1)}, f32[8,128]{1,0:T(8,128)S(1)}) custom-call(f32[512,4096]{1,0:T(8,128)S(1)} %copy-done.1, f32[512,128]{1,0:T(8,128)S(1)} %get-tuple-element.42.cosine_ref, f32[512,128]{1,0:T(8,128)S(1)} %get-tuple-element.43.sine_ref, f32[2,128]{1,0:T(2,128)S(1)} %convert_element_type.87.gains_ref, ...), custom_call_target="tpu_custom_call" | custom-call | flops 4294967296 | bytes 16777216 | tf_op jit(solution)/shard_map/attention_back/pallas_call | solution.py:181
  410.8 7.0 convolution_convert_fusion.1
  419.4 12.8 %convolution_convert_fusion = bf16[1024,6144]{1,0:T(8,128)(2,1)} fusion(bf16[512,3072]{1,0:T(8,128)(2,1)} %get-tuple-element.21, bf16[512,3072]{1,0:T(8,128)(2,1)} %get-tuple-element.20, f32[512,1024]{1,0:T(8,128)S(1)} %copy-done.8, f32[1024]{0:T(1024)S(1)} %bitcast.77, f32[512]{0:T(512)S(1)} %get-tuple-element.37), kind=kOutput, calls=%fused_computation | convolution fusion | flops 6462898176 | bytes 20977664 | tf_op jit(solution)/shard_map/dot_general | solution.py:25
  432.3 11.1 %fusion.9 = (f32[1024]{0:T(1024)S(1)}, f32[512]{0:T(512)S(1)}, f32[512,1024]{1,0:T(8,128)}) fusion(bf16[512,1024]{1,0:T(8,128)(2,1)} %param.13, f32[512]{0:T(512)S(1)} %get-tuple-element.35, f32[1024]{0:T(1024)S(1)} %bitcast.72, bf16[512,4096]{1,0:T(8,128)(2,1)} %copy-done.2, bf16[1024,4096]{1,0:T(8,128)(2,1)} %all-gather.6.cloned.1.call-done), kind=kOutput, calls=%fused_computation.26 | convolution fusion | flops 4298635776 | bytes 15740928 | tf_op jit(solution)/shard_map/dot_general | solution.py:25
  443.4 40.0 %psum.7 = f32[2304]{0:T(1024)S(1)} all-reduce(f32[2304]{0:T(1024)S(1)} %pad_maximum_fusion.7), channel_id=1, replica_groups=mesh['fsdp'=8,'rep'=4] {'fsdp','rep'}, use_global_device_ids=true, to_apply=%region_8.9 | all-reduce | flops 2304 | bytes 18432 | tf_op jit(solution)/shard_map/psum | solution.py:300
  488.2 7.2 add_convert_fusion
  495.4 11.0 %reduce-scatter.7.cloned.1.call-done = bf16[64,1024]{1,0:T(8,128)(2,1)} async-done(((bf16[2048,1024]{1,0:T(8,128)(2,1)}), bf16[64,1024]{1,0:T(8,128)(2,1)}) %reduce-scatter.7.cloned.1.call-update) | async-done | bytes 131088 | tf_op jit(solution)/shard_map/reduce_scatter | solution.py:38
  508.0 117.0 %reduce-scatter.11.cloned.1.call-done = bf16[96,1024]{1,0:T(8,128)(2,1)} async-done(((bf16[3072,1024]{1,0:T(8,128)(2,1)}), bf16[96,1024]{1,0:T(8,128)(2,1)}) %reduce-scatter.11.cloned.1.call-update) | async-done | bytes 196624 | tf_op jit(solution)/shard_map/reduce_scatter | solution.py:38
  626.7 185.8 %reduce-scatter.5.cloned.1.call-done = bf16[32,4096]{1,0:T(8,128)(2,1)} async-done(((bf16[1024,4096]{1,0:T(8,128)(2,1)}), bf16[32,4096]{1,0:T(8,128)(2,1)}) %reduce-scatter.5.cloned.1.call-update) | async-done | bytes 262160 | tf_op jit(solution)/shard_map/reduce_scatter | solution.py:38
  815.8 156.9 %reduce-scatter.9.cloned.1.call-done = bf16[32,6144]{1,0:T(8,128)(2,1)} async-done(((bf16[1024,6144]{1,0:T(8,128)(2,1)}), bf16[32,6144]{1,0:T(8,128)(2,1)}) %reduce-scatter.9.cloned.1.call-update) | async-done | bytes 393232 | tf_op jit(solution)/shard_map/reduce_scatter | solution.py:38
  (84 shorter events, 37.0 us)
Async XLA Ops:
  7.2 6.9 copy-start.10
  7.2 6.9 copy-start.11
  7.2 76.9 %copy-start.12 = (bf16[2,128]{1,0:T(2,128)(2,1)S(1)}, bf16[2,128]{1,0:T(2,128)(2,1)}, u32[]{:S(2)}) copy-start(bf16[2,128]{1,0:T(2,128)(2,1)} %param.20) | copy-start | bytes 1540
  7.2 76.9 %copy-start.13 = (s32[1,4]{1,0:T(1,128)S(1)}, s32[1,4]{1,0:T(1,128)}, u32[]{:S(2)}) copy-start(s32[1,4]{1,0:T(1,128)} %param.14) | copy-start | bytes 52
  7.2 78.5 %copy-start.5 = (bf16[512,1024]{1,0:T(8,128)(2,1)S(1)}, bf16[512,1024]{1,0:T(8,128)(2,1)}, u32[]{:S(2)}) copy-start(bf16[512,1024]{1,0:T(8,128)(2,1)} %param.13) | copy-start | bytes 3145732
  7.2 84.7 %all-gather.6.cloned.1.call-start = ((), (), s32[]{:S(2)}) async-start(), calls=%async_computation.4 | async-start | bytes 8650752 | tf_op jit(solution)/shard_map/all_gather | solution.py:34
  10.8 144.8 %all-gather.8.cloned.1.call-start = ((), (), s32[]{:S(2)}) async-start(), calls=%async_computation.5 | async-start | bytes 4325376 | tf_op jit(solution)/shard_map/all_gather | solution.py:34
  11.6 242.1 %all-gather.10.cloned.1.call-start = ((), (), s32[]{:S(2)}) async-start(), calls=%async_computation.6 | async-start | bytes 12976128 | tf_op jit(solution)/shard_map/all_gather | solution.py:34
  13.5 310.9 %all-gather.12.cloned.1.call-start = ((), (), s32[]{:S(2)}) async-start(), calls=%async_computation.7 | async-start | bytes 6488064 | tf_op jit(solution)/shard_map/all_gather | solution.py:34
  14.0 492.3 %reduce-scatter.7.cloned.1.call-start = ((), (), s32[]{:S(2)}) async-start(), calls=%async_computation.9 | async-start | bytes 4325376 | tf_op jit(solution)/shard_map/reduce_scatter | solution.py:38
  125.1 3.2 copy-start
  354.5 1.3 copy-start.3
  360.3 264.7 %reduce-scatter.11.cloned.1.call-start = ((), (), s32[]{:S(2)}) async-start(), calls=%async_computation.11 | async-start | bytes 6488064 | tf_op jit(solution)/shard_map/reduce_scatter | solution.py:38
  368.7 443.8 %reduce-scatter.5.cloned.1.call-start = ((), (), s32[]{:S(2)}) async-start(), calls=%async_computation.8 | async-start | bytes 8650752 | tf_op jit(solution)/shard_map/reduce_scatter | solution.py:38
  373.9 3.4 copy-start.1
  377.4 33.4 %copy-start.6 = (bf16[512,1024]{1,0:T(8,128)(2,1)S(1)}, bf16[512,1024]{1,0:T(8,128)(2,1)}, u32[]{:S(2)}) copy-start(bf16[512,1024]{1,0:T(8,128)(2,1)} %param.13) | copy-start | bytes 3145732
  408.7 2.1 copy-start.2
  417.8 1.6 copy-start.8
  417.8 554.8 %reduce-scatter.9.cloned.1.call-start = ((), (), s32[]{:S(2)}) async-start(), calls=%async_computation.10 | async-start | bytes 12976128 | tf_op jit(solution)/shard_map/reduce_scatter | solution.py:38
  432.3 52.3 %copy-start.4 = (f32[512,1024]{1,0:T(8,128)S(1)}, f32[512,1024]{1,0:T(8,128)}, u32[]{:S(2)}) copy-start(f32[512,1024]{1,0:T(8,128)} %copy-done.3) | copy-start | bytes 6291460
  432.3 52.3 %copy-start.7 = (bf16[512,1024]{1,0:T(8,128)(2,1)S(1)}, bf16[512,1024]{1,0:T(8,128)(2,1)}, u32[]{:S(2)}) copy-start(bf16[512,1024]{1,0:T(8,128)(2,1)} %param.13) | copy-start | bytes 3145732
  484.6 3.6 copy-start.9
  484.6 3.6 copy-start.14
Sparse Core Ops, SparseCore 0:
  11.6 80.2 all-gather.5
  94.9 60.7 all-gather.7
  159.1 94.5 all-gather.9
  256.5 67.7 all-gather.11
  360.4 145.9 reduce-scatter.6
  511.9 113.0 reduce-scatter.10
  627.4 185.1 reduce-scatter.4
  819.6 153.0 reduce-scatter.8

commit v2 on v1

--- a/solution.py
+++ b/solution.py
@@ -34,8 +34,54 @@
     return lax.all_gather(block, AXES, axis=0, tiled=True)
 
 
-def scatter_sum(values):
-    return lax.psum_scatter(values, AXES, scatter_dimension=0, tiled=True)
+def mesh_bits():
+    bits = []
+    for axis in AXES:
+        step = lax.axis_size(axis) // 2
+        while step > 0:
+            bits.append((axis, step))
+            step //= 2
+    return bits
+
+
+def swap(values, axis, step):
+    pairs = [(here, here ^ step) for here in range(lax.axis_size(axis))]
+    return lax.ppermute(values, axis, pairs)
+
+
+def bit_of(axis, step):
+    return (lax.axis_index(axis) // step) % 2
+
+
+def exchange_order(turn):
+    bits = mesh_bits()
+    last = [bit for bit in bits if bit[0] == AXES[1] and bit[1] > 1]
+    middle = [bit for bit in bits if bit not in last and bit != (AXES[0], 1)]
+    turn = turn % len(middle)
+    return [(AXES[0], 1)] + middle[turn:] + middle[:turn] + last
+
+
+def scatter_sum(values, turn):
+    left = mesh_bits()
+    order = exchange_order(turn)
+    width = values.shape[1]
+    for axis, step in order:
+        place = left.index((axis, step))
+        left.remove((axis, step))
+        halves = values.reshape(2**place, 2, -1, width)
+        bit = bit_of(axis, step)
+        mine = lax.dynamic_index_in_dim(halves, bit, 1, keepdims=False)
+        other = lax.dynamic_index_in_dim(halves, 1 - bit, 1, keepdims=False)
+        total = high(mine) + high(swap(other, axis, step))
+        values = low(total) if left else total
+        values = values.reshape(-1, width)
+    return values
+
+
+def sum_all(values):
+    for axis, step in mesh_bits():
+        values = values + swap(values, axis, step)
+    return values
 
 
 def head_norm_rope(raw, gain, cosine, sine):
@@ -279,26 +325,34 @@
     mixed = low(gate_silu * up)
     layer_out = low(middle + dot(mixed, back_weight, NN))
 
-    down_sum = scatter_sum(low(dot(mixed, cotangent, TN)))
+    down_sum = scatter_sum(low(dot(mixed, cotangent, TN)), 0)
     dmixed = dot(cotangent, back_weight, NT)
     dgate = low(dmixed * up * (gate_sigmoid + gate_silu * (1.0 - gate_sigmoid)))
     dup = low(dmixed * gate_silu)
+    gate_sum = scatter_sum(low(dot(normed_two, dgate, TN)), 1)
+    up_sum = scatter_sum(low(dot(normed_two, dup, TN)), 2)
     dpair = jnp.concatenate([dgate, dup], axis=1)
-    pair_sum = scatter_sum(low(dot(normed_two, dpair, TN)))
     dnormed_two = dot(dpair, pair_weight, NT)
     dmiddle, mlp_norm_grad = norm_back(middle, rate_two, gain_two, dnormed_two)
     dmiddle = high(cotangent) + dmiddle
     dbranch = low(dmiddle)
-    out_sum = scatter_sum(low(dot(attended, dbranch, TN)))
+    out_sum = scatter_sum(low(dot(attended, dbranch, TN)), 0)
     dattended = low(dot(dbranch, out_weight, NT))
     dqkv, gains_grad = attention_back(qkv, *tables, attended, dattended, group)
-    qkv_sum = scatter_sum(low(dot(normed_one, dqkv, TN)))
+    half = dqkv.shape[1] // 2
+    qkv_sum = jnp.concatenate(
+        [
+            scatter_sum(low(dot(normed_one, dqkv[:, :half], TN)), 1),
+            scatter_sum(low(dot(normed_one, dqkv[:, half:], TN)), 2),
+        ],
+        axis=1,
+    )
     dnormed_one = dot(dqkv, qkv_weight, NT)
     dinputs, attn_norm_grad = norm_back(inputs, rate_one, gain_one, dnormed_one)
     input_grad = dmiddle + dinputs
 
-    small = lax.psum(
-        jnp.concatenate([attn_norm_grad, mlp_norm_grad, gains_grad[:2].reshape(-1)]), AXES
+    small = sum_all(
+        jnp.concatenate([attn_norm_grad, mlp_norm_grad, gains_grad[:2].reshape(-1)])
     )
     width = attn_norm_grad.shape[0]
     place = (lax.axis_index("fsdp") * lax.axis_size("rep") + lax.axis_index("rep")) * own
@@ -306,11 +360,10 @@
     mlp_norm_sum = lax.dynamic_slice(small, (width + place,), (own,))
     gains_sum = small[2 * width :].reshape(2, size)
 
-    qkv_sum = high(qkv_sum).reshape(own, kv_heads, -1)
+    qkv_sum = qkv_sum.reshape(own, kv_heads, -1)
     q_sum = qkv_sum[:, :, : group * size].reshape(own, -1)
     k_sum = qkv_sum[:, :, group * size : (group + 1) * size].reshape(own, -1)
     v_sum = qkv_sum[:, :, (group + 1) * size :].reshape(own, -1)
-    pair_sum = high(pair_sum)
     return (
         layer_out,
         input_grad,
@@ -318,12 +371,12 @@
         q_sum,
         k_sum,
         v_sum,
-        high(out_sum),
+        out_sum,
         gains_sum,
         mlp_norm_sum,
-        pair_sum[:, :hidden],
-        pair_sum[:, hidden:],
-        high(down_sum),
+        gate_sum,
+        up_sum,
+        down_sum,
     )
 
 

time: 991 us -> 664 us (0.67)
  waiting for transfers between devices: 653 us -> 305 us
  blocking collectives: 110 us -> 69.8 us
  starting transfers between devices: 0.32 us -> 36.8 us
  other arithmetic: 13.7 us -> 41.5 us
  local copies, waits for them, and re-layouts: 21.6 us -> 33.4 us
    reduce_scatter x4 -> x0, waiting for transfers between devices: 471 us -> none  [scatter_sum(): return lax.psum_scatter(values, AXES, scatter_dimension=0, tiled=True)]
    ppermute x0 -> x35, waiting for transfers between devices: none -> 122 us  [swap(): return lax.ppermute(values, axis, pairs)]
    psum x1 -> x0, blocking collectives: 40 us -> none  [local(): lax.psum(jnp.concatenate([attn_norm_grad, mlp_norm_grad, gains_grad[:2].r...]
    ppermute x0 -> x35, starting transfers between devices: none -> 36.6 us  [swap(): return lax.ppermute(values, axis, pairs)]
    convert_element_type x0 -> x25, other arithmetic: none -> 24.4 us  [low(): return values.astype(jnp.bfloat16)]
    squeeze x0 -> x30, local copies, waits for them, and re-layouts: none -> 17 us  [scatter_sum(): other = lax.dynamic_index_in_dim(halves, 1 - bit, 1, keepdims=False)]
    dot_general x12 -> x14, matrix products: 111 us -> 102 us  [dot(): lax.dot_general(left, right, (dims, ((), ())), preferred_element_type=jnp...]
  transfers between devices with their start and end apart: 8 -> 39, of which waited for: 8 -> 22; matrix products, arithmetic and copies ran while one was open for 10% -> 15% of each run, Pallas kernels for 6% -> 4%
where the time goes in v2:
time: 664 us; the launch traced here: 661 us
  waiting for transfers between devices  305 us (46%)
  matrix products  102 us (15%)
  blocking collectives  69.8 us (11%)
  Pallas kernels  57.5 us (9%)
  other arithmetic  41.5 us (6%)
  starting transfers between devices  36.8 us (6%)
  local copies, waits for them, and re-layouts  33.4 us (5%)
  between operations  15 us (2%)
    all_gather x4, waiting for transfers between devices, gather(): return lax.all_gather(block, AXES, axis=0, tiled=True)  181 us
    ppermute x35, waiting for transfers between devices, swap(): return lax.ppermute(values, axis, pairs)  122 us
    dot_general x14, matrix products, dot(): lax.dot_general(left, right, (dims, ((), ())), preferred_element_type=jnp...  102 us
    all_gather x1, blocking collectives, gather(): return lax.all_gather(block, AXES, axis=0, tiled=True)  69.8 us
    ppermute x35, starting transfers between devices, swap(): return lax.ppermute(values, axis, pairs)  36.6 us
    pallas_call x1, Pallas kernels, attention_back(): pl.pallas_call(functools.partial(attention_back_kernel, group), grid=(hea...  31.5 us
    pallas_call x1, Pallas kernels, attention(): pl.pallas_call(functools.partial(attention_kernel, group), grid=(heads,),...  26 us
    convert_element_type x25, other arithmetic, low(): return values.astype(jnp.bfloat16)  24.4 us
  transfers between devices with their start and end apart: 39, of which 22 were waited for; matrix products, arithmetic and copies ran while one was open for 15% of the time, Pallas kernels for 4%

profile of v2, /device:TPU:0, one launch (start us, length us, event | category | flops | bytes accessed | tf_op | source)
XLA Modules:
  0.0 661.3 jit_solution(3816372820825189228)
XLA Ops:
  14.2 69.8 %all-gather = bf16[32,32,2]{1,2,0:T(2,128)(2,1)S(1)} all-gather(bf16[1,32,2]{1,2,0:T(2,128)(2,1)S(1)} %maximum_bitcast_fusion), channel_id=1, replica_groups=mesh['fsdp'=8,'rep'=4] {'fsdp','rep'}, dimensions={0}, use_global_device_ids=true | all-gather | bytes 4224 | tf_op jit(solution)/shard_map/all_gather | solution.py:34
  86.2 5.8 all-gather.6.cloned.1.call-done
  91.9 7.4 %fusion.50.qkv_ref = f32[512,4096]{1,0:T(8,128)S(1)} fusion(bf16[1024,4096]{1,0:T(8,128)(2,1)} %all-gather.6.cloned.1.call-done, bf16[512,1024]{1,0:T(8,128)(2,1)S(1)} %copy-done.12, f32[1024]{0:T(1024)S(1)} %bitcast.309, f32[512]{0:T(512)S(1)} %get-tuple-element.33), kind=kOutput, calls=%fused_computation.161 | convolution fusion | flops 4297064448 | bytes 17831936 | tf_op jit(solution)/shard_map/dot_general | solution.py:25
  99.3 26.0 %attention.1.out_ref = bf16[512,2048]{1,0:T(8,128)(2,1)S(1)} custom-call(f32[512,4096]{1,0:T(8,128)S(1)} %fusion.50.qkv_ref, f32[512,128]{1,0:T(8,128)S(1)} %get-tuple-element.40.cosine_ref, f32[512,128]{1,0:T(8,128)S(1)} %get-tuple-element.41.sine_ref, f32[2,128]{1,0:T(2,128)S(1)} %convert_element_type.535.gains_ref, s32[512,1]{1,0:T(8,128)S(1)} %copy.35.start_ref), custom_call_target="tpu_custom_call" | custom-call | flops 1610612736 | bytes 10485760 | tf_op jit(solution)/shard_map/attention/pallas_call | solution.py:206
  128.6 27.2 %all-gather.8.cloned.1.call-done = bf16[2048,1024]{1,0:T(8,128)(2,1)} async-done(((bf16[64,1024]{1,0:T(8,128)(2,1)}), bf16[2048,1024]{1,0:T(8,128)(2,1)}) %all-gather.8.cloned.1.call-update) | async-done | bytes 4194320 | tf_op jit(solution)/shard_map/all_gather | solution.py:34
  155.7 5.0 multiply_reduce_fusion.2
  163.2 90.6 %all-gather.10.cloned.1.call-done = bf16[1024,6144]{1,0:T(8,128)(2,1)} async-done(((bf16[32,6144]{1,0:T(8,128)(2,1)}), bf16[1024,6144]{1,0:T(8,128)(2,1)}) %all-gather.10.cloned.1.call-update) | async-done | bytes 12582928 | tf_op jit(solution)/shard_map/all_gather | solution.py:34
  253.8 12.6 %fusion.53 = f32[512,6144]{1,0:T(8,128)} fusion(bf16[512,1024]{1,0:T(8,128)(2,1)} %multiply_convert_fusion.3, bf16[1024,6144]{1,0:T(8,128)(2,1)} %all-gather.10.cloned.1.call-done), kind=kOutput, calls=%fused_computation.163 | convolution fusion | flops 6442450944 | bytes 26214400 | tf_op jit(solution)/shard_map/dot_general | solution.py:25
  266.5 57.9 %all-gather.12.cloned.1.call-done = bf16[3072,1024]{1,0:T(8,128)(2,1)} async-done(((bf16[96,1024]{1,0:T(8,128)(2,1)}), bf16[3072,1024]{1,0:T(8,128)(2,1)}) %all-gather.12.cloned.1.call-update) | async-done | bytes 6291472 | tf_op jit(solution)/shard_map/all_gather | solution.py:34
  324.4 12.8 %multiply_convert_fusion.1 = (bf16[512,3072]{1,0:T(8,128)(2,1)}, bf16[512,3072]{1,0:T(8,128)(2,1)}, bf16[512,3072]{1,0:T(8,128)(2,1)}) fusion(f32[512,6144]{1,0:T(8,128)} %fusion.53, bf16[512,1024]{1,0:T(8,128)(2,1)} %param.25, bf16[3072,1024]{1,0:T(8,128)(2,1)} %all-gather.12.cloned.1.call-done), kind=kOutput, calls=%fused_computation.11 | convolution fusion | flops 3243245568 | bytes 29360128 | tf_op jit(solution)/shard_map/dot_general | solution.py:25
  337.2 14.7 %multiply_reduce_fusion = (f32[1024]{0:T(1024)S(1)}, f32[512]{0:T(512)S(1)}, f32[512,1024]{1,0:T(8,128)}) fusion(f32[512,1024]{1,0:T(8,128)} %copy-done.5, f32[512]{0:T(512)S(1)} %get-tuple-element.35, f32[1024]{0:T(1024)S(1)} %bitcast.306, bf16[1024,6144]{1,0:T(8,128)(2,1)} %all-gather.10.cloned.1.call-done, bf16[512,3072]{1,0:T(8,128)(2,1)} %get-tuple-element.21, ...), kind=kOutput, calls=%fused_computation.63 | convolution fusion | flops 6458178048 | bytes 23080960 | tf_op jit(solution)/shard_map/dot_general | solution.py:25
  355.1 4.7 convolution_convert_fusion.6.dout_ref
  359.9 31.5 %attention_back.1 = (bf16[512,4096]{1,0:T(8,128)(2,1)S(1)}, f32[8,128]{1,0:T(8,128)S(1)}) custom-call(f32[512,4096]{1,0:T(8,128)S(1)} %bitcast.232, f32[512,128]{1,0:T(8,128)S(1)} %get-tuple-element.40.cosine_ref, f32[512,128]{1,0:T(8,128)S(1)} %get-tuple-element.41.sine_ref, f32[2,128]{1,0:T(2,128)S(1)} %convert_element_type.535.gains_ref, ...), custom_call_target="tpu_custom_call" | custom-call | flops 4294967296 | bytes 16777216 | tf_op jit(solution)/shard_map/attention_back/pallas_call | solution.py:227
  395.9 4.6 convolution_convert_fusion.4
  412.5 9.6 %fusion.21 = (f32[1024]{0:T(1024)S(1)}, f32[512]{0:T(512)S(1)}, f32[512,1024]{1,0:T(8,128)}) fusion(bf16[512,1024]{1,0:T(8,128)(2,1)S(1)} %copy-done.14, f32[512]{0:T(512)S(1)} %get-tuple-element.33, f32[1024]{0:T(1024)S(1)} %bitcast.312, bf16[512,4096]{1,0:T(8,128)(2,1)S(1)} %get-tuple-element.14, bf16[1024,4096]{1,0:T(8,128)(2,1)} %all-gather.6.cloned.1.call-done), kind=kOutput, calls=%fused_computation.51 | convolution fusion | flops 4298635776 | bytes 15740928 | tf_op jit(solution)/shard_map/dot_general | solution.py:25
  434.2 10.4 %add_convert_fusion = bf16[512,1024]{1,0:T(8,128)(2,1)} fusion(f32[512,1024]{1,0:T(8,128)S(1)} %copy-done.6, bf16[512,3072]{1,0:T(8,128)(2,1)} %get-tuple-element.22, bf16[3072,1024]{1,0:T(8,128)(2,1)} %all-gather.12.cloned.1.call-done), kind=kOutput, calls=%fused_computation.66 | convolution fusion | flops 3222274048 | bytes 12582912 | tf_op jit(solution)/shard_map/dot_general | solution.py:25
  470.6 18.9 %collective-permute-done.6 = bf16[2,128,2048]{2,1,0:T(8,128)(2,1)S(1)} collective-permute-done((bf16[2,128,2048]{2,1,0:T(8,128)(2,1)S(1)}, bf16[2,128,2048]{2,1,0:T(8,128)(2,1)S(1)}, u32[]{:S(2)}, u32[]{:S(2)}) %collective-permute-start.6) | collective-permute-done | bytes 1048608 | tf_op jit(solution)/shard_map/ppermute | solution.py:49
  493.7 20.1 %collective-permute-done.16 = bf16[1,512,1024]{2,1,0:T(8,128)(2,1)S(1)} collective-permute-done((bf16[1,512,1024]{2,1,0:T(8,128)(2,1)S(1)}, bf16[1,512,1024]{2,1,0:T(8,128)(2,1)S(1)}, u32[]{:S(2)}, u32[]{:S(2)}) %collective-permute-start.16) | collective-permute-done | bytes 1048608 | tf_op jit(solution)/shard_map/ppermute | solution.py:49
  536.6 35.8 %collective-permute-done.8 = bf16[1,64,2048]{2,1,0:T(8,128)(2,1)S(1)} collective-permute-done((bf16[1,64,2048]{2,1,0:T(8,128)(2,1)S(1)}, bf16[1,64,2048]{2,1,0:T(8,128)(2,1)S(1)}, u32[]{:S(2)}, u32[]{:S(2)}) %collective-permute-start.8) | collective-permute-done | bytes 262176 | tf_op jit(solution)/shard_map/ppermute | solution.py:49
  575.7 4.6 collective-permute-done.18
  608.1 9.5 %collective-permute-done.22 = bf16[4,32,3072]{2,1,0:T(8,128)(2,1)S(1)} collective-permute-done((bf16[4,32,3072]{2,1,0:T(8,128)(2,1)S(1)}, bf16[4,32,3072]{2,1,0:T(8,128)(2,1)S(1)}, u32[]{:S(2)}, u32[]{:S(2)}) %collective-permute-start.22) | collective-permute-done | bytes 786464 | tf_op jit(solution)/shard_map/ppermute | solution.py:49
  618.9 4.6 collective-permute-done.27
  634.3 5.1 collective-permute-done.33
  640.8 6.3 collective-permute-done.24
  (241 shorter events, 150.9 us)
Async XLA Ops:
  7.2 84.7 %all-gather.6.cloned.1.call-start = ((), (), s32[]{:S(2)}) async-start(), calls=%async_computation | async-start | bytes 8650752 | tf_op jit(solution)/shard_map/all_gather | solution.py:34
  10.8 144.9 %all-gather.8.cloned.1.call-start = ((), (), s32[]{:S(2)}) async-start(), calls=%async_computation.1 | async-start | bytes 4325376 | tf_op jit(solution)/shard_map/all_gather | solution.py:34
  11.6 242.2 %all-gather.10.cloned.1.call-start = ((), (), s32[]{:S(2)}) async-start(), calls=%async_computation.2 | async-start | bytes 12976128 | tf_op jit(solution)/shard_map/all_gather | solution.py:34
  13.5 310.9 %all-gather.12.cloned.1.call-start = ((), (), s32[]{:S(2)}) async-start(), calls=%async_computation.3 | async-start | bytes 6488064 | tf_op jit(solution)/shard_map/all_gather | solution.py:34
  422.1 24.6 %collective-permute-start = (f32[2304]{0:T(1024)S(1)}, f32[2304]{0:T(1024)S(1)}, u32[]{:S(2)}, u32[]{:S(2)}) collective-permute-start(f32[2304]{0:T(1024)S(1)} %pad_maximum_fusion.5), channel_id=1, source_target_pairs={{0,16},{4,20},{8,24},{12,28},{16,0},{20,4},{24,8},{28,12},{1,17},{... | collective-permute-start | bytes 27656 | tf_op jit(solution)/shard_map/ppermute | solution.py:49
  426.7 36.3 %collective-permute-start.5 = (bf16[4,128,2048]{2,1,0:T(8,128)(2,1)}, bf16[4,128,2048]{2,1,0:T(8,128)(2,1)S(1)}, u32[]{:S(2)}, u32[]{:S(2)}) collective-permute-start(bf16[4,128,2048]{2,1,0:T(8,128)(2,1)} %dynamic-slice_bitcast_fusion.5), channel_id=1, source_target_pairs={{0,4},{4,0},{8,12},{12,8},{16,20},{20,16},{24,28},{28,24},{1,5},{5... | collective-permute-start | bytes 6291464 | tf_op jit(solution)/shard_map/ppermute | solution.py:49
  446.1 18.3 %collective-permute-start.10 = (bf16[4,128,2048]{2,1,0:T(8,128)(2,1)}, bf16[4,128,2048]{2,1,0:T(8,128)(2,1)S(1)}, u32[]{:S(2)}, u32[]{:S(2)}) collective-permute-start(bf16[4,128,2048]{2,1,0:T(8,128)(2,1)} %dynamic-slice_bitcast_fusion.4), channel_id=1, source_target_pairs={{0,4},{4,0},{8,12},{12,8},{16,20},{20,16},{24,28},{28,24},{1,5},{5... | collective-permute-start | bytes 6291464 | tf_op jit(solution)/shard_map/ppermute | solution.py:49
  450.7 64.5 %collective-permute-start.20 = (bf16[4,128,3072]{2,1,0:T(8,128)(2,1)S(1)}, bf16[4,128,3072]{2,1,0:T(8,128)(2,1)}, u32[]{:S(2)}, u32[]{:S(2)}) collective-permute-start(bf16[4,128,3072]{2,1,0:T(8,128)(2,1)S(1)} %dynamic-slice_bitcast_fusion.2), channel_id=1, source_target_pairs={{0,4},{4,0},{8,12},{12,8},{16,20},{20,16},{24,28},{28,24},{1,5},{5... | collective-permute-start | bytes 9437192 | tf_op jit(solution)/shard_map/ppermute | solution.py:49
  461.8 58.8 %collective-permute-start.25 = (bf16[4,128,3072]{2,1,0:T(8,128)(2,1)}, bf16[4,128,3072]{2,1,0:T(8,128)(2,1)}, u32[]{:S(2)}, u32[]{:S(2)}) collective-permute-start(bf16[4,128,3072]{2,1,0:T(8,128)(2,1)} %dynamic-slice_bitcast_fusion.1), channel_id=1, source_target_pairs={{0,4},{4,0},{8,12},{12,8},{16,20},{20,16},{24,28},{28,24},{1,5},{5... | collective-permute-start | bytes 9437192 | tf_op jit(solution)/shard_map/ppermute | solution.py:49
  463.0 63.4 %collective-permute-start.30 = (bf16[4,384,1024]{2,1,0:T(8,128)(2,1)}, bf16[4,384,1024]{2,1,0:T(8,128)(2,1)}, u32[]{:S(2)}, u32[]{:S(2)}) collective-permute-start(bf16[4,384,1024]{2,1,0:T(8,128)(2,1)} %dynamic-slice_bitcast_fusion), channel_id=1, source_target_pairs={{0,4},{4,0},{8,12},{12,8},{16,20},{20,16},{24,28},{28,24},{1,5},{5... | collective-permute-start | bytes 9437192 | tf_op jit(solution)/shard_map/ppermute | solution.py:49
  464.4 25.1 %collective-permute-start.6 = (bf16[2,128,2048]{2,1,0:T(8,128)(2,1)S(1)}, bf16[2,128,2048]{2,1,0:T(8,128)(2,1)S(1)}, u32[]{:S(2)}, u32[]{:S(2)}) collective-permute-start(bf16[2,128,2048]{2,1,0:T(8,128)(2,1)S(1)} %dynamic-slice_bitcast_fusion.11), channel_id=1, source_target_pairs={{0,8},{4,12},{8,0},{12,4},{16,24},{20,28},{24,16},{28,20},{1,9},{5... | collective-permute-start | bytes 3145736 | tf_op jit(solution)/shard_map/ppermute | solution.py:49
  466.4 25.4 %collective-permute-start.11 = (bf16[8,32,2048]{2,1,0:T(8,128)(2,1)S(1)}, bf16[8,32,2048]{2,1,0:T(8,128)(2,1)S(1)}, u32[]{:S(2)}, u32[]{:S(2)}) collective-permute-start(bf16[8,32,2048]{2,1,0:T(8,128)(2,1)S(1)} %dynamic-slice_bitcast_fusion.10), channel_id=1, source_target_pairs={{0,1},{1,0},{2,3},{3,2},{4,5},{5,4},{6,7},{7,6},{8,9},{9,8},{10,11... | collective-permute-start | bytes 3145736 | tf_op jit(solution)/shard_map/ppermute | solution.py:49
  489.5 24.2 %collective-permute-start.16 = (bf16[1,512,1024]{2,1,0:T(8,128)(2,1)S(1)}, bf16[1,512,1024]{2,1,0:T(8,128)(2,1)S(1)}, u32[]{:S(2)}, u32[]{:S(2)}) collective-permute-start(bf16[1,512,1024]{2,1,0:T(8,128)(2,1)S(1)} %dynamic-slice_bitcast_fusion.9), channel_id=1, source_target_pairs={{0,16},{4,20},{8,24},{12,28},{16,0},{20,4},{24,8},{28,12},{1,17},{... | collective-permute-start | bytes 3145736 | tf_op jit(solution)/shard_map/ppermute | solution.py:49
  491.7 41.1 %collective-permute-start.7 = (bf16[4,32,2048]{2,1,0:T(8,128)(2,1)S(1)}, bf16[4,32,2048]{2,1,0:T(8,128)(2,1)S(1)}, u32[]{:S(2)}, u32[]{:S(2)}) collective-permute-start(bf16[4,32,2048]{2,1,0:T(8,128)(2,1)S(1)} %dynamic-slice_bitcast_fusion.17), channel_id=1, source_target_pairs={{0,1},{1,0},{2,3},{3,2},{4,5},{5,4},{6,7},{7,6},{8,9},{9,8},{10,11... | collective-permute-start | bytes 1572872 | tf_op jit(solution)/shard_map/ppermute | solution.py:49
  513.8 20.3 %collective-permute-start.12 = (bf16[1,128,2048]{2,1,0:T(8,128)(2,1)S(1)}, bf16[1,128,2048]{2,1,0:T(8,128)(2,1)S(1)}, u32[]{:S(2)}, u32[]{:S(2)}) collective-permute-start(bf16[1,128,2048]{2,1,0:T(8,128)(2,1)S(1)} %dynamic-slice_bitcast_fusion.16), channel_id=1, source_target_pairs={{0,16},{4,20},{8,24},{12,28},{16,0},{20,4},{24,8},{28,12},{1,17},{... | collective-permute-start | bytes 1572872 | tf_op jit(solution)/shard_map/ppermute | solution.py:49
  515.2 20.1 %collective-permute-start.17 = (bf16[1,256,1024]{2,1,0:T(8,128)(2,1)S(1)}, bf16[1,256,1024]{2,1,0:T(8,128)(2,1)S(1)}, u32[]{:S(2)}, u32[]{:S(2)}) collective-permute-start(bf16[1,256,1024]{2,1,0:T(8,128)(2,1)S(1)} %dynamic-slice_bitcast_fusion.15), channel_id=1, source_target_pairs={{0,8},{4,12},{8,0},{12,4},{16,24},{20,28},{24,16},{28,20},{1,9},{5... | collective-permute-start | bytes 1572872 | tf_op jit(solution)/shard_map/ppermute | solution.py:49
  520.6 78.5 %collective-permute-start.21 = (bf16[2,128,3072]{2,1,0:T(8,128)(2,1)}, bf16[2,128,3072]{2,1,0:T(8,128)(2,1)}, u32[]{:S(2)}, u32[]{:S(2)}) collective-permute-start(bf16[2,128,3072]{2,1,0:T(8,128)(2,1)} %dynamic-slice_bitcast_fusion.8), channel_id=1, source_target_pairs={{0,8},{4,12},{8,0},{12,4},{16,24},{20,28},{24,16},{28,20},{1,9},{5... | collective-permute-start | bytes 4718600 | tf_op jit(solution)/shard_map/ppermute | solution.py:49
  526.3 75.1 %collective-permute-start.26 = (bf16[8,32,3072]{2,1,0:T(8,128)(2,1)}, bf16[8,32,3072]{2,1,0:T(8,128)(2,1)}, u32[]{:S(2)}, u32[]{:S(2)}) collective-permute-start(bf16[8,32,3072]{2,1,0:T(8,128)(2,1)} %dynamic-slice_bitcast_fusion.7), channel_id=1, source_target_pairs={{0,1},{1,0},{2,3},{3,2},{4,5},{5,4},{6,7},{7,6},{8,9},{9,8},{10,11... | collective-permute-start | bytes 4718600 | tf_op jit(solution)/shard_map/ppermute | solution.py:49
  532.8 72.0 %collective-permute-start.31 = (bf16[1,768,1024]{2,1,0:T(8,128)(2,1)}, bf16[1,768,1024]{2,1,0:T(8,128)(2,1)}, u32[]{:S(2)}, u32[]{:S(2)}) collective-permute-start(bf16[1,768,1024]{2,1,0:T(8,128)(2,1)} %dynamic-slice_bitcast_fusion.6), channel_id=1, source_target_pairs={{0,16},{4,20},{8,24},{12,28},{16,0},{20,4},{24,8},{28,12},{1,17},{... | collective-permute-start | bytes 4718600 | tf_op jit(solution)/shard_map/ppermute | solution.py:49
  534.1 38.3 %collective-permute-start.8 = (bf16[1,64,2048]{2,1,0:T(8,128)(2,1)S(1)}, bf16[1,64,2048]{2,1,0:T(8,128)(2,1)S(1)}, u32[]{:S(2)}, u32[]{:S(2)}) collective-permute-start(bf16[1,64,2048]{2,1,0:T(8,128)(2,1)S(1)} %dynamic-slice_bitcast_fusion.23), channel_id=1, source_target_pairs={{0,16},{4,20},{8,24},{12,28},{16,0},{20,4},{24,8},{28,12},{1,17},{... | collective-permute-start | bytes 786440 | tf_op jit(solution)/shard_map/ppermute | solution.py:49
  535.3 37.7 %collective-permute-start.13 = (bf16[1,64,2048]{2,1,0:T(8,128)(2,1)S(1)}, bf16[1,64,2048]{2,1,0:T(8,128)(2,1)S(1)}, u32[]{:S(2)}, u32[]{:S(2)}) collective-permute-start(bf16[1,64,2048]{2,1,0:T(8,128)(2,1)S(1)} %dynamic-slice_bitcast_fusion.22), channel_id=1, source_target_pairs={{0,8},{4,12},{8,0},{12,4},{16,24},{20,28},{24,16},{28,20},{1,9},{5... | collective-permute-start | bytes 786440 | tf_op jit(solution)/shard_map/ppermute | solution.py:49
  603.7 19.8 %collective-permute-start.27 = (bf16[1,128,3072]{2,1,0:T(8,128)(2,1)S(1)}, bf16[1,128,3072]{2,1,0:T(8,128)(2,1)S(1)}, u32[]{:S(2)}, u32[]{:S(2)}) collective-permute-start(bf16[1,128,3072]{2,1,0:T(8,128)(2,1)S(1)} %dynamic-slice_bitcast_fusion.13), channel_id=1, source_target_pairs={{0,16},{4,20},{8,24},{12,28},{16,0},{20,4},{24,8},{28,12},{1,17},{... | collective-permute-start | bytes 2359304 | tf_op jit(solution)/shard_map/ppermute | solution.py:49
  607.0 20.2 %collective-permute-start.32 = (bf16[1,384,1024]{2,1,0:T(8,128)(2,1)S(1)}, bf16[1,384,1024]{2,1,0:T(8,128)(2,1)S(1)}, u32[]{:S(2)}, u32[]{:S(2)}) collective-permute-start(bf16[1,384,1024]{2,1,0:T(8,128)(2,1)S(1)} %dynamic-slice_bitcast_fusion.12), channel_id=1, source_target_pairs={{0,8},{4,12},{8,0},{12,4},{16,24},{20,28},{24,16},{28,20},{1,9},{5... | collective-permute-start | bytes 2359304 | tf_op jit(solution)/shard_map/ppermute | solution.py:49
  631.7 19.6 %collective-permute-start.29 = (bf16[1,32,3072]{2,1,0:T(8,128)(2,1)S(1)}, bf16[1,32,3072]{2,1,0:T(8,128)(2,1)S(1)}, u32[]{:S(2)}, u32[]{:S(2)}) collective-permute-start(bf16[1,32,3072]{2,1,0:T(8,128)(2,1)S(1)} %dynamic-slice_bitcast_fusion.24), channel_id=1, source_target_pairs={{0,2},{1,3},{2,0},{3,1},{4,6},{5,7},{6,4},{7,5},{8,10},{9,11},{10,... | collective-permute-start | bytes 589832 | tf_op jit(solution)/shard_map/ppermute | solution.py:49
  (46 other events, 566.3 us)
Sparse Core Ops, SparseCore 0:
  11.6 80.2 all-gather.5
  94.9 60.8 all-gather.7
  159.2 94.5 all-gather.9
  256.6 67.7 all-gather.11
